TPU v7x, 512 devices: a whole 4x4x16 slice. The times are simulated.
512 devices in a mesh: slab: 32 (over y, x, core), tile: 16 (over z).
Axes of the slice: x: 4, y: 4, z: 16, core: 2. Of those that a mesh axis runs over, the one named last changes fastest.
Arguments:
- history: bfloat16 [32, 2048, 8, 128], P('slab', 'tile'), may hold values from -15 to 15
- positions: bfloat16 [32, 2048, 3, 128], P('slab', 'tile'), may hold values from 0 to 1
- kappa_old: float32 [32, 2048, 128], P('slab', 'tile'), may hold values from 0.2 to 2
- threshold: float32 [32, 2048, 128], P('slab', 'tile'), may hold values from 0.3 to 1.5
- pair_ids: int32 [32, 2048, 8], P('slab', 'tile'), may hold values from 0 to 2047, as said below
- reader_counts: int32 [32, 2048], P('slab', 'tile'), may hold values from 1 to 8, as said below
- brick_map: int32 [32, 2048], P('slab', 'tile'), may hold values from 0 to 511, as said below
- strain_disp: bfloat16 [1024, 128], replicated, may hold values from -0.1875 to 0.1875
- couple: float32 [128, 128], replicated, may hold values from -0.5 to 0.5
Outputs:
- damage: float32 [32, 2048, 128], P('slab', 'tile')
- residual: float32 [1024, 16, 128], P('slab', 'tile')
Inputs may be any that keep to these rules, and one draw needn't show every extreme that they name: pair_ids[s, r, 0] = r; the other sources may be any clusters of the same depth layer. Only the first reader_counts[s, r] entries of pair_ids[s, r] are used. `brick_map`: a cluster among clusters t * 128 to (t + 1) * 128 - 1 lies in a brick among bricks (t - 1) * 32 to (t + 2) * 32 - 1.
All inputs are finite; a program needn't handle non-finite values.
Results may differ from a plain program's by a relative error of at most 0.0054.
Values may be sent and summed in bfloat16 or wider, within the bound.
No kernel may reach another device: no remote copies, remote signals or barrier semaphores. Data moves between devices by JAX's collectives and lax.ppermute only.
A program may use at most 64 MiB of HBM per device.

v0:
```python
import jax
import jax.numpy as jnp
from jax import lax
from jax.sharding import PartitionSpec as P

PAIRS = 8
BR_DEV = 32
SHARP = 12.0
SOFTEN = 2.0


def passed_along(block, axis, distance):
    devices = range(lax.axis_size(axis))
    route = [(i - distance, i) for i in devices if i - distance in devices]
    return lax.ppermute(block, axis, route)


def padded_2(array, sides, width):
    for axis, dim in sides:
        peers, length = (lax.axis_size(axis), array.shape[dim])
        up = [(i, (i + 1) % peers) for i in range(peers - 1)]
        down = [(j, i) for i, j in up]
        last = lax.slice_in_dim(array, length - width, length, axis=dim)
        leading = lax.slice_in_dim(array, 0, width, axis=dim)
        before = lax.ppermute(last, axis, up)
        after = lax.ppermute(leading, axis, down)
        array = jnp.concatenate([before, array, after], axis=dim)
    return array


def local(
    history,
    positions,
    kappa_old,
    threshold,
    pair_ids,
    reader_counts,
    brick_map,
    strain_disp,
    couple,
):
    hist = history[0]
    clusters = hist.shape[0]
    columns = hist.shape[1]
    points = hist.shape[2]
    packed = jnp.concatenate([hist, positions[0]], axis=1)
    tile_at = lax.axis_index("tile")
    ids = pair_ids[0]
    source = lax.all_gather(packed, "tile", axis=0, tiled=True)
    blocks = jnp.take(source, ids, axis=0)
    here = positions[0].astype(jnp.float32)
    counts = reader_counts[0]
    numer = jnp.zeros((clusters, columns, points), jnp.float32)
    denom = jnp.zeros((clusters, points), jnp.float32)
    for entry in range(PAIRS):
        src_hist = blocks[:, entry, :columns, :]
        src_pos = blocks[:, entry, columns:, :].astype(jnp.float32)
        dist = jnp.zeros((clusters, points, points), jnp.float32)
        for axis_k in range(3):
            delta = here[:, axis_k, :, None] - src_pos[:, axis_k, None, :]
            dist = dist + delta * delta
        live = (entry < counts).astype(jnp.float32)[:, None, None]
        weight = (jnp.exp(-SHARP * dist) * live).astype(jnp.bfloat16)
        numer = numer + jnp.einsum(
            "rcj,rij->rci", src_hist, weight, preferred_element_type=jnp.float32
        )
        denom = denom + jnp.sum(weight.astype(jnp.float32), axis=2)
    averaged = numer / denom[:, None, :]
    kappa = jnp.maximum(jnp.maximum(kappa_old[0], averaged[:, 0, :]), threshold[0])
    damage_here = 1.0 - threshold[0] / kappa * jnp.exp(-(kappa - threshold[0]) / SOFTEN)
    effective = ((1.0 - damage_here)[:, None, :] * averaged).astype(jnp.bfloat16)
    term = jnp.dot(
        effective.reshape(clusters, columns * points),
        strain_disp,
        preferred_element_type=jnp.float32,
    )
    bricks = BR_DEV
    owner = brick_map[0]
    local_brick = owner - (tile_at - 1) * bricks
    rows_near = lax.iota(jnp.int32, 3 * bricks)
    onehot = (local_brick[None, :] == rows_near[:, None]).astype(jnp.float32)
    shares = jnp.dot(
        onehot, term, precision=lax.Precision.HIGHEST, preferred_element_type=jnp.float32
    )
    shares = shares.reshape(3, bricks, term.shape[1])
    from_lower = passed_along(shares[2], "tile", 1)
    from_upper = passed_along(shares[0], "tile", -1)
    force = shares[1] + from_lower + from_upper
    padded = padded_2(force, (("slab", 0),), 1)
    beside = padded[:-2] + padded[2:]
    residual_here = force + jnp.dot(
        beside, couple, precision=lax.Precision.HIGHEST, preferred_element_type=jnp.float32
    )
    return (damage_here[None, :, :], residual_here[:, None, :])


def solution(mesh):
    placed = (
        P("slab", "tile", None, None),
        P("slab", "tile", None, None),
        P("slab", "tile", None),
        P("slab", "tile", None),
        P("slab", "tile", None),
        P("slab", "tile"),
        P("slab", "tile"),
        P(),
        P(),
    )
    return jax.shard_map(
        local,
        mesh=mesh,
        in_specs=placed,
        out_specs=(P("slab", "tile", None), P("slab", "tile", None)),
        check_vma=False,
    )
```

profile of v0, /device:TPU:7, one launch (start us, length us, event | category | flops | bytes accessed | tf_op | source)
XLA Modules:
  0.0 307.6 jit_solution(755815150721862255)
XLA Ops:
  7.2 1.0 copy.83
  8.2 1.7 pad_maximum_fusion
  9.9 0.7 compare_select_fusion
  10.8 0.7 subtract_bitcast_fusion
  11.5 0.7 fusion.36
  12.1 0.7 compare_and_fusion
  12.8 0.9 bitcast_convert_fusion
  13.8 79.4 %all-gather.2.cloned.1.call-done = bf16[2048,11,128]{2,0,1:T(8,128)(2,1)} async-done(((bf16[128,11,128]{2,0,1:T(8,128)(2,1)}), bf16[2048,11,128]{2,0,1:T(8,128)(2,1)}) %all-gather.2.cloned.1.call-update) | async-done | bytes 5767184 | tf_op jit(solution)/shard_map/all_gather | solution.py:49
  93.2 9.0 %copy.44 = bf16[2048,11,128]{2,1,0:T(8,128)(2,1)} copy(bf16[2048,11,128]{2,0,1:T(8,128)(2,1)} %all-gather.2.cloned.1.call-done) | data formatting | bytes 11534336 | tf_op jit(solution)/shard_map/all_gather | solution.py:49
  102.2 11.9 %gather_fusion = bf16[1024,11,128]{2,1,0:T(8,128)(2,1)} fusion(bf16[2048,11,128]{2,1,0:T(8,128)(2,1)} %copy.44, s32[1024]{0:T(1024)S(1)} %broadcast_clamp_fusion), kind=kCustom, calls=%fused_computation | custom fusion | bytes 5771264 | tf_op jit(solution)/shard_map/jit(_take)/gather | solution.py:50
  114.1 3.6 %copy_select_fusion = bf16[128,8,11,128]{3,2,0,1:T(8,128)(2,1)S(1)} fusion(bf16[128,8,11,128]{3,2,1,0:T(8,128)(2,1)} %bitcast.146, pred[128,8]{0,1:T(8,128)(4,1)S(1)} %compare_and_fusion), kind=kLoop, calls=%fused_computation.17 | loop fusion | flops 1441792 | bytes 5768192 | tf_op jit(solution)/shard_map/jit(_take)/select_n | solution.py:50
  117.7 0.3 fusion.16
  118.9 13.0 %fusion = f32[128,8,128]{2,1,0:T(8,128)S(1)} fusion(f32[128]{0:T(128)S(1)} %get-tuple-element.61, f32[128,128]{1,0:T(8,128)S(1)} %bitcast.164, f32[128,128]{1,0:T(8,128)S(1)} %get-tuple-element.55, f32[128,128]{1,0:T(8,128)S(1)} %bitcast.166, f32[128,128]{1,0:T(8,128)S(1)} %get-tuple-element.56, f32[128,128]{1,0:T(8,128)S(1)} %bitcast.162, ...), kind=kOutput, calls=%fused_computation.18 | convolution fusion | flops 56623104 | bytes 1180160 | tf_op jit(solution)/shard_map/rcj,rij->rci/dot_general | solution.py:64
  131.9 13.0 %fusion.2 = f32[128,8,128]{2,1,0:T(8,128)S(1)} fusion(f32[128]{0:T(128)S(1)} %get-tuple-element.65, f32[128,128]{1,0:T(8,128)S(1)} %bitcast.176, f32[128,128]{1,0:T(8,128)S(1)} %bitcast.178, f32[128,128]{1,0:T(8,128)S(1)} %bitcast.174, f32[128,128]{1,0:T(8,128)S(1)} %get-tuple-element.55, f32[128,128]{1,0:T(8,128)S(1)} %get-tuple-element.56, ...), kind=kOutput, calls=%fused_computation.20 | convolution fusion | flops 56623104 | bytes 1180160 | tf_op jit(solution)/shard_map/rcj,rij->rci/dot_general | solution.py:64
  144.9 13.0 %fusion.3 = f32[128,8,128]{2,1,0:T(8,128)S(1)} fusion(f32[128]{0:T(128)S(1)} %get-tuple-element.64, f32[128,128]{1,0:T(8,128)S(1)} %bitcast.182, f32[128,128]{1,0:T(8,128)S(1)} %bitcast.180, f32[128,128]{1,0:T(8,128)S(1)} %bitcast.184, f32[128,128]{1,0:T(8,128)S(1)} %get-tuple-element.55, f32[128,128]{1,0:T(8,128)S(1)} %get-tuple-element.56, ...), kind=kOutput, calls=%fused_computation.21 | convolution fusion | flops 56623104 | bytes 1180160 | tf_op jit(solution)/shard_map/rcj,rij->rci/dot_general | solution.py:64
  157.9 25.4 %convert_reduce_fusion.7 = (f32[128,128]{1,0:T(8,128)S(1)}, f32[128,128]{1,0:T(8,128)S(1)}, f32[128,128]{1,0:T(8,128)S(1)}, f32[128,128]{1,0:T(8,128)S(1)}) fusion(f32[128]{0:T(128)S(1)} %get-tuple-element.61, f32[128,128]{1,0:T(8,128)S(1)} %bitcast.165, f32[128,128]{1,0:T(8,128)S(1)} %get-tuple-element.55, f32[128,128]{1,0:T(8,128)S(1)} %bitcast.167, ...), kind=kLoop, calls=%fused_computation.8 | loop fusion | flops 108986368 | bytes 1247232 | tf_op jit(solution)/shard_map/reduce_sum | solution.py:67
  183.3 13.0 %fusion.4 = f32[128,8,128]{2,1,0:T(8,128)S(1)} fusion(f32[128]{0:T(128)S(1)} %get-tuple-element.63, f32[128,128]{1,0:T(8,128)S(1)} %bitcast.189, f32[128,128]{1,0:T(8,128)S(1)} %bitcast.191, f32[128,128]{1,0:T(8,128)S(1)} %bitcast.187, f32[128,128]{1,0:T(8,128)S(1)} %get-tuple-element.55, f32[128,128]{1,0:T(8,128)S(1)} %get-tuple-element.56, ...), kind=kOutput, calls=%fused_computation.22 | convolution fusion | flops 56623104 | bytes 1180160 | tf_op jit(solution)/shard_map/rcj,rij->rci/dot_general | solution.py:64
  196.3 0.3 fusion.59
  196.6 13.0 %fusion.1 = f32[128,8,128]{2,1,0:T(8,128)S(1)} fusion(f32[128]{0:T(128)S(1)} %get-tuple-element.66, f32[128,128]{1,0:T(8,128)S(1)} %bitcast.152, f32[128,128]{1,0:T(8,128)S(1)} %bitcast.150, f32[128,128]{1,0:T(8,128)S(1)} %bitcast.154, f32[128,128]{1,0:T(8,128)S(1)} %get-tuple-element.55, f32[128,128]{1,0:T(8,128)S(1)} %get-tuple-element.56, ...), kind=kOutput, calls=%fused_computation.19 | convolution fusion | flops 56623104 | bytes 1180160 | tf_op jit(solution)/shard_map/rcj,rij->rci/dot_general | solution.py:64
  209.5 13.0 %fusion.5 = f32[128,8,128]{2,1,0:T(8,128)S(1)} fusion(f32[128]{0:T(128)S(1)} %get-tuple-element.62, f32[128,128]{1,0:T(8,128)S(1)} %bitcast.158, f32[128,128]{1,0:T(8,128)S(1)} %bitcast.156, f32[128,128]{1,0:T(8,128)S(1)} %bitcast.160, f32[128,128]{1,0:T(8,128)S(1)} %get-tuple-element.55, f32[128,128]{1,0:T(8,128)S(1)} %get-tuple-element.56, ...), kind=kOutput, calls=%fused_computation.23 | convolution fusion | flops 56623104 | bytes 1180160 | tf_op jit(solution)/shard_map/rcj,rij->rci/dot_general | solution.py:64
  222.5 13.0 %fusion.6 = f32[128,8,128]{2,1,0:T(8,128)S(1)} fusion(f32[128]{0:T(128)S(1)} %get-tuple-element.68, f32[128,128]{1,0:T(8,128)S(1)} %bitcast.194, f32[128,128]{1,0:T(8,128)S(1)} %bitcast.196, f32[128,128]{1,0:T(8,128)S(1)} %bitcast.192, f32[128,128]{1,0:T(8,128)S(1)} %get-tuple-element.55, f32[128,128]{1,0:T(8,128)S(1)} %get-tuple-element.56, ...), kind=kOutput, calls=%fused_computation.24 | convolution fusion | flops 56623104 | bytes 1180160 | tf_op jit(solution)/shard_map/rcj,rij->rci/dot_general | solution.py:64
  235.5 25.4 %convert_reduce_fusion.6 = (f32[128,128]{1,0:T(8,128)S(1)}, f32[128,128]{1,0:T(8,128)S(1)}, f32[128,128]{1,0:T(8,128)S(1)}, f32[128,128]{1,0:T(8,128)S(1)}) fusion(f32[128]{0:T(128)S(1)} %get-tuple-element.66, f32[128,128]{1,0:T(8,128)S(1)} %bitcast.153, f32[128,128]{1,0:T(8,128)S(1)} %get-tuple-element.55, f32[128,128]{1,0:T(8,128)S(1)} %bitcast.151, ...), kind=kLoop, calls=%fused_computation.7 | loop fusion | flops 108986368 | bytes 1247232 | tf_op jit(solution)/shard_map/reduce_sum | solution.py:67
  261.0 13.0 %fusion.7 = f32[128,8,128]{2,1,0:T(8,128)S(1)} fusion(f32[128]{0:T(128)S(1)} %get-tuple-element.67, f32[128,128]{1,0:T(8,128)S(1)} %bitcast.171, f32[128,128]{1,0:T(8,128)S(1)} %bitcast.169, f32[128,128]{1,0:T(8,128)S(1)} %bitcast.173, f32[128,128]{1,0:T(8,128)S(1)} %get-tuple-element.55, f32[128,128]{1,0:T(8,128)S(1)} %get-tuple-element.56, ...), kind=kOutput, calls=%fused_computation.25 | convolution fusion | flops 56623104 | bytes 1180160 | tf_op jit(solution)/shard_map/rcj,rij->rci/dot_general | solution.py:64
  274.0 0.6 fusion.8
  275.4 3.0 collective-permute-start
  278.3 1.3 collective-permute-start.1
  279.6 3.2 %collective-permute-done.1 = f32[32,128]{1,0:T(8,128)S(1)} collective-permute-done((f32[32,128]{1,0:T(8,128)S(1)}, f32[32,128]{1,0:T(8,128)S(1)}, u32[]{:S(2)}, u32[]{:S(2)}) %collective-permute-start.1) | collective-permute-done | bytes 16416 | tf_op jit(solution)/shard_map/ppermute | solution.py:15
  282.8 10.2 %collective-permute-start.2 = (f32[1,128]{1,0:T(1,128)S(1)}, f32[1,128]{1,0:T(1,128)S(1)}, u32[]{:S(2)}, u32[]{:S(2)}) collective-permute-start(f32[1,128]{1,0:T(1,128)S(1)} %get-tuple-element.59), channel_id=1, source_target_pairs={{0,16},{16,32},{32,48},{48,64},{64,80},{80,96},{96,112},{112,128},... | collective-permute-start | bytes 1544 | tf_op jit(solution)/shard_map/ppermute | solution.py:25
  293.0 1.9 collective-permute-start.3
  294.9 0.7 fusion.18
  295.6 4.4 %collective-permute-done.3 = f32[1,128]{1,0:T(1,128)S(1)} collective-permute-done((f32[1,128]{1,0:T(1,128)S(1)}, f32[1,128]{1,0:T(1,128)S(1)}, u32[]{:S(2)}, u32[]{:S(2)}) %collective-permute-start.3) | collective-permute-done | bytes 544 | tf_op jit(solution)/shard_map/ppermute | solution.py:26
  300.0 0.8 convolution_add_fusion
  (28 shorter events, 1.9 us)
Async XLA Ops:
  7.2 267.7 %copy-start = (bf16[1024,128]{1,0:T(8,128)(2,1)S(1)}, bf16[1024,128]{1,0:T(8,128)(2,1)}, u32[]{:S(2)}) copy-start(bf16[1024,128]{1,0:T(8,128)(2,1)} %param.16) | copy-start | bytes 786436
  7.2 86.0 %all-gather.2.cloned.1.call-start = ((), (), s32[]{:S(2)}) async-start(), calls=%async_computation | async-start | bytes 6127616 | tf_op jit(solution)/shard_map/all_gather | solution.py:49
  260.9 13.7 %copy-start.1 = (f32[1,128,128]{2,1,0:T(8,128)S(1)}, f32[1,128,128]{2,1,0:T(8,128)}, u32[]{:S(2)}) copy-start(f32[1,128,128]{2,1,0:T(8,128)} %param.12) | copy-start | bytes 196612
  260.9 13.7 %copy-start.2 = (f32[1,128,128]{2,1,0:T(8,128)S(1)}, f32[1,128,128]{2,1,0:T(8,128)}, u32[]{:S(2)}) copy-start(f32[1,128,128]{2,1,0:T(8,128)} %param.11) | copy-start | bytes 196612
  260.9 39.0 %copy-start.3 = (f32[128,128]{1,0:T(8,128)S(1)}, f32[128,128]{1,0:T(8,128)}, u32[]{:S(2)}) copy-start(f32[128,128]{1,0:T(8,128)} %param.17) | copy-start | bytes 196612
  275.4 4.3 %collective-permute-start = (f32[32,128]{1,0:T(8,128)S(1)}, f32[32,128]{1,0:T(8,128)S(1)}, u32[]{:S(2)}, u32[]{:S(2)}) collective-permute-start(f32[32,128]{1,0:T(8,128)S(1)} %get-tuple-element.57), channel_id=1, source_target_pairs={{0,1},{1,2},{2,3},{3,4},{4,5},{5,6},{6,7},{7,8},{8,9},{9,10},{10,1... | collective-permute-start | bytes 49160 | tf_op jit(solution)/shard_map/ppermute | solution.py:15
  278.3 4.5 %collective-permute-start.1 = (f32[32,128]{1,0:T(8,128)S(1)}, f32[32,128]{1,0:T(8,128)S(1)}, u32[]{:S(2)}, u32[]{:S(2)}) collective-permute-start(f32[32,128]{1,0:T(8,128)S(1)} %get-tuple-element.58), channel_id=1, source_target_pairs={{1,0},{2,1},{3,2},{4,3},{5,4},{6,5},{7,6},{8,7},{9,8},{10,9},{11,1... | collective-permute-start | bytes 49160 | tf_op jit(solution)/shard_map/ppermute | solution.py:15
  282.8 12.8 %collective-permute-start.2 = (f32[1,128]{1,0:T(1,128)S(1)}, f32[1,128]{1,0:T(1,128)S(1)}, u32[]{:S(2)}, u32[]{:S(2)}) collective-permute-start(f32[1,128]{1,0:T(1,128)S(1)} %get-tuple-element.59), channel_id=1, source_target_pairs={{0,16},{16,32},{32,48},{48,64},{64,80},{80,96},{96,112},{112,128},... | collective-permute-start | bytes 1544 | tf_op jit(solution)/shard_map/ppermute | solution.py:25
  293.0 7.0 %collective-permute-start.3 = (f32[1,128]{1,0:T(1,128)S(1)}, f32[1,128]{1,0:T(1,128)S(1)}, u32[]{:S(2)}, u32[]{:S(2)}) collective-permute-start(f32[1,128]{1,0:T(1,128)S(1)} %get-tuple-element.60), channel_id=1, source_target_pairs={{16,0},{32,16},{48,32},{64,48},{80,64},{96,80},{112,96},{128,112},... | collective-permute-start | bytes 1544 | tf_op jit(solution)/shard_map/ppermute | solution.py:26
Sparse Core Ops, SparseCore 0:
  10.1 83.0 all-gather.1
where the time goes:
time: 308 us
  matrix products  105 us (34%)
  waiting for transfers between devices  87 us (28%)
  other arithmetic  61.5 us (20%)
  local copies, waits for them, and re-layouts  23.4 us (8%)
  starting transfers between devices  16.4 us (5%)
  between operations  14.3 us (5%)
    dot_general x8, matrix products, local(): jnp.einsum('rcj,rij->rci', src_hist, weight, preferred_element_type=jnp.f...  104 us
    all_gather x1, waiting for transfers between devices, local(): source = lax.all_gather(packed, 'tile', axis=0, tiled=True)  79.4 us
    reduce_sum x2, other arithmetic, local(): denom = denom + jnp.sum(weight.astype(jnp.float32), axis=2)  50.8 us
    gather x1, local copies, waits for them, and re-layouts, local(): blocks = jnp.take(source, ids, axis=0)  11.9 us
    ppermute x1, starting transfers between devices, padded_2(): before = lax.ppermute(last, axis, up)  10.2 us
    all_gather x1, local copies, waits for them, and re-layouts, local(): source = lax.all_gather(packed, 'tile', axis=0, tiled=True)  9.01 us
  transfers between devices with their start and end apart: 5, of which 3 were waited for; matrix products, arithmetic and copies ran while one was open for 1% of the time, Pallas kernels for 0%

commit v1 on v0

--- a/solution.py
+++ b/solution.py
@@ -46,7 +46,9 @@
     packed = jnp.concatenate([hist, positions[0]], axis=1)
     tile_at = lax.axis_index("tile")
     ids = pair_ids[0]
-    source = lax.all_gather(packed, "tile", axis=0, tiled=True)
+    source = jnp.concatenate(
+        lax.all_to_all(jnp.stack([packed] * lax.axis_size("tile")), "tile", 0, 0), axis=0
+    )
     blocks = jnp.take(source, ids, axis=0)
     here = positions[0].astype(jnp.float32)
     counts = reader_counts[0]

time: 308 us -> 478 us (1.55)
  waiting for transfers between devices: 87 us -> 256 us
  between operations: 14.3 us -> 1 us
  starting transfers between devices: 16.4 us -> 28.4 us
  local copies, waits for them, and re-layouts: 23.4 us -> 29.2 us
    all_to_all x0 -> x1, waiting for transfers between devices: none -> 249 us  [local(): lax.all_to_all(jnp.stack([packed] * lax.axis_size('tile')), 'tile', 0, 0)]
    all_gather x1 -> x0, waiting for transfers between devices: 79.4 us -> none  [local(): source = lax.all_gather(packed, 'tile', axis=0, tiled=True)]
    all_to_all x0 -> x1, starting transfers between devices: none -> 15 us  [local(): lax.all_to_all(jnp.stack([packed] * lax.axis_size('tile')), 'tile', 0, 0)]
    all_to_all x0 -> x1, local copies, waits for them, and re-layouts: none -> 10.8 us  [local(): lax.all_to_all(jnp.stack([packed] * lax.axis_size('tile')), 'tile', 0, 0)]
    all_gather x1 -> x0, local copies, waits for them, and re-layouts: 9.01 us -> none  [local(): source = lax.all_gather(packed, 'tile', axis=0, tiled=True)]
  transfers between devices with their start and end apart: 5 -> 5, of which waited for: 3 -> 3; matrix products, arithmetic and copies ran while one was open for 1% -> 0% of each run, Pallas kernels for 0% -> 0%
where the time goes in v1:
time: 478 us; the launch traced here: 477 us
  waiting for transfers between devices  256 us (54%)
  matrix products  105 us (22%)
  other arithmetic  57.5 us (12%)
  local copies, waits for them, and re-layouts  29.2 us (6%)
  starting transfers between devices  28.4 us (6%)
    all_to_all x1, waiting for transfers between devices, local(): lax.all_to_all(jnp.stack([packed] * lax.axis_size('tile')), 'tile', 0, 0)  249 us
    dot_general x8, matrix products, local(): jnp.einsum('rcj,rij->rci', src_hist, weight, preferred_element_type=jnp.f...  104 us
    reduce_sum x2, other arithmetic, local(): denom = denom + jnp.sum(weight.astype(jnp.float32), axis=2)  51 us
    all_to_all x1, starting transfers between devices, local(): lax.all_to_all(jnp.stack([packed] * lax.axis_size('tile')), 'tile', 0, 0)  15 us
    gather x1, local copies, waits for them, and re-layouts, local(): blocks = jnp.take(source, ids, axis=0)  11.8 us
    all_to_all x1, local copies, waits for them, and re-layouts, local(): lax.all_to_all(jnp.stack([packed] * lax.axis_size('tile')), 'tile', 0, 0)  10.8 us
  transfers between devices with their start and end apart: 5, of which 3 were waited for; matrix products, arithmetic and copies ran while one was open for 0% of the time, Pallas kernels for 0%

profile of v1, /device:TPU:7, one launch (start us, length us, event | category | flops | bytes accessed | tf_op | source)
XLA Modules:
  0.0 477.5 jit_solution(17441480228001423938)
XLA Ops:
  0.6 1.0 copy.44
  1.7 1.1 pad_maximum_fusion
  2.9 3.9 stack.2
  6.8 15.0 %all-to-all-start = ((bf16[16,128,11,128]{3,1,2,0:T(8,128)(2,1)}), bf16[16,128,11,128]{3,1,2,0:T(8,128)(2,1)}, u32[]{:S(2)}, u32[]{:S(2)}) async-start(bf16[16,128,11,128]{3,1,2,0:T(8,128)(2,1)} %stack.2), calls=%async_computation | async-start | bytes 11534336 | tf_op jit(solution)/shard_map/all_to_all | solution.py:50
  22.2 248.9 %all-to-all-done = bf16[16,128,11,128]{3,1,2,0:T(8,128)(2,1)} async-done(((bf16[16,128,11,128]{3,1,2,0:T(8,128)(2,1)}), bf16[16,128,11,128]{3,1,2,0:T(8,128)(2,1)}, u32[]{:S(2)}, u32[]{:S(2)}) %all-to-all-start) | async-done | bytes 5767200 | tf_op jit(solution)/shard_map/all_to_all | solution.py:50
  271.0 10.8 %copy.46 = bf16[16,128,11,128]{3,2,1,0:T(8,128)(2,1)} copy(bf16[16,128,11,128]{3,1,2,0:T(8,128)(2,1)} %all-to-all-done) | data formatting | bytes 11534336 | tf_op jit(solution)/shard_map/all_to_all | solution.py:50
  281.8 11.8 %gather_fusion = bf16[1024,11,128]{2,1,0:T(8,128)(2,1)} fusion(bf16[2048,11,128]{2,1,0:T(8,128)(2,1)} %bitcast.145, s32[1024]{0:T(1024)S(1)} %broadcast_clamp_fusion), kind=kCustom, calls=%fused_computation | custom fusion | bytes 5771264 | tf_op jit(solution)/shard_map/jit(_take)/gather | solution.py:52
  293.6 3.6 copy_select_fusion
  297.2 0.3 fusion.16
  297.6 0.3 fusion.53
  297.8 0.3 fusion.55
  298.1 0.3 fusion.57
  298.4 13.0 %fusion = f32[128,8,128]{2,1,0:T(8,128)S(1)} fusion(f32[128]{0:T(128)S(1)} %get-tuple-element.61, f32[128,128]{1,0:T(8,128)S(1)} %bitcast.164, f32[128,128]{1,0:T(8,128)S(1)} %get-tuple-element.55, f32[128,128]{1,0:T(8,128)S(1)} %bitcast.166, f32[128,128]{1,0:T(8,128)S(1)} %get-tuple-element.56, f32[128,128]{1,0:T(8,128)S(1)} %bitcast.162, ...), kind=kOutput, calls=%fused_computation.18 | convolution fusion | flops 56623104 | bytes 1180160 | tf_op jit(solution)/shard_map/rcj,rij->rci/dot_general | solution.py:66
  311.4 13.0 %fusion.2 = f32[128,8,128]{2,1,0:T(8,128)S(1)} fusion(f32[128]{0:T(128)S(1)} %get-tuple-element.65, f32[128,128]{1,0:T(8,128)S(1)} %bitcast.176, f32[128,128]{1,0:T(8,128)S(1)} %bitcast.178, f32[128,128]{1,0:T(8,128)S(1)} %bitcast.174, f32[128,128]{1,0:T(8,128)S(1)} %get-tuple-element.55, f32[128,128]{1,0:T(8,128)S(1)} %get-tuple-element.56, ...), kind=kOutput, calls=%fused_computation.20 | convolution fusion | flops 56623104 | bytes 1180160 | tf_op jit(solution)/shard_map/rcj,rij->rci/dot_general | solution.py:66
  324.4 13.0 %fusion.3 = f32[128,8,128]{2,1,0:T(8,128)S(1)} fusion(f32[128]{0:T(128)S(1)} %get-tuple-element.64, f32[128,128]{1,0:T(8,128)S(1)} %bitcast.182, f32[128,128]{1,0:T(8,128)S(1)} %bitcast.180, f32[128,128]{1,0:T(8,128)S(1)} %bitcast.184, f32[128,128]{1,0:T(8,128)S(1)} %get-tuple-element.55, f32[128,128]{1,0:T(8,128)S(1)} %get-tuple-element.56, ...), kind=kOutput, calls=%fused_computation.21 | convolution fusion | flops 56623104 | bytes 1180160 | tf_op jit(solution)/shard_map/rcj,rij->rci/dot_general | solution.py:66
  337.3 25.4 %convert_reduce_fusion.7 = (f32[128,128]{1,0:T(8,128)S(1)}, f32[128,128]{1,0:T(8,128)S(1)}, f32[128,128]{1,0:T(8,128)S(1)}, f32[128,128]{1,0:T(8,128)S(1)}) fusion(f32[128]{0:T(128)S(1)} %get-tuple-element.61, f32[128,128]{1,0:T(8,128)S(1)} %bitcast.165, f32[128,128]{1,0:T(8,128)S(1)} %get-tuple-element.55, f32[128,128]{1,0:T(8,128)S(1)} %bitcast.167, ...), kind=kLoop, calls=%fused_computation.8 | loop fusion | flops 108986368 | bytes 1247232 | tf_op jit(solution)/shard_map/reduce_sum | solution.py:69
  362.8 13.0 %fusion.4 = f32[128,8,128]{2,1,0:T(8,128)S(1)} fusion(f32[128]{0:T(128)S(1)} %get-tuple-element.63, f32[128,128]{1,0:T(8,128)S(1)} %bitcast.189, f32[128,128]{1,0:T(8,128)S(1)} %bitcast.191, f32[128,128]{1,0:T(8,128)S(1)} %bitcast.187, f32[128,128]{1,0:T(8,128)S(1)} %get-tuple-element.55, f32[128,128]{1,0:T(8,128)S(1)} %get-tuple-element.56, ...), kind=kOutput, calls=%fused_computation.22 | convolution fusion | flops 56623104 | bytes 1180160 | tf_op jit(solution)/shard_map/rcj,rij->rci/dot_general | solution.py:66
  375.8 0.3 fusion.59
  376.0 13.0 %fusion.1 = f32[128,8,128]{2,1,0:T(8,128)S(1)} fusion(f32[128]{0:T(128)S(1)} %get-tuple-element.66, f32[128,128]{1,0:T(8,128)S(1)} %bitcast.152, f32[128,128]{1,0:T(8,128)S(1)} %bitcast.150, f32[128,128]{1,0:T(8,128)S(1)} %bitcast.154, f32[128,128]{1,0:T(8,128)S(1)} %get-tuple-element.55, f32[128,128]{1,0:T(8,128)S(1)} %get-tuple-element.56, ...), kind=kOutput, calls=%fused_computation.19 | convolution fusion | flops 56623104 | bytes 1180160 | tf_op jit(solution)/shard_map/rcj,rij->rci/dot_general | solution.py:66
  389.0 13.0 %fusion.5 = f32[128,8,128]{2,1,0:T(8,128)S(1)} fusion(f32[128]{0:T(128)S(1)} %get-tuple-element.62, f32[128,128]{1,0:T(8,128)S(1)} %bitcast.158, f32[128,128]{1,0:T(8,128)S(1)} %bitcast.156, f32[128,128]{1,0:T(8,128)S(1)} %bitcast.160, f32[128,128]{1,0:T(8,128)S(1)} %get-tuple-element.55, f32[128,128]{1,0:T(8,128)S(1)} %get-tuple-element.56, ...), kind=kOutput, calls=%fused_computation.23 | convolution fusion | flops 56623104 | bytes 1180160 | tf_op jit(solution)/shard_map/rcj,rij->rci/dot_general | solution.py:66
  402.0 13.0 %fusion.6 = f32[128,8,128]{2,1,0:T(8,128)S(1)} fusion(f32[128]{0:T(128)S(1)} %get-tuple-element.68, f32[128,128]{1,0:T(8,128)S(1)} %bitcast.194, f32[128,128]{1,0:T(8,128)S(1)} %bitcast.196, f32[128,128]{1,0:T(8,128)S(1)} %bitcast.192, f32[128,128]{1,0:T(8,128)S(1)} %get-tuple-element.55, f32[128,128]{1,0:T(8,128)S(1)} %get-tuple-element.56, ...), kind=kOutput, calls=%fused_computation.24 | convolution fusion | flops 56623104 | bytes 1180160 | tf_op jit(solution)/shard_map/rcj,rij->rci/dot_general | solution.py:66
  415.0 25.6 %convert_reduce_fusion.6 = (f32[128,128]{1,0:T(8,128)S(1)}, f32[128,128]{1,0:T(8,128)S(1)}, f32[128,128]{1,0:T(8,128)S(1)}, f32[128,128]{1,0:T(8,128)S(1)}) fusion(f32[128]{0:T(128)S(1)} %get-tuple-element.66, f32[128,128]{1,0:T(8,128)S(1)} %bitcast.153, f32[128,128]{1,0:T(8,128)S(1)} %get-tuple-element.55, f32[128,128]{1,0:T(8,128)S(1)} %bitcast.151, ...), kind=kLoop, calls=%fused_computation.7 | loop fusion | flops 108986368 | bytes 1247232 | tf_op jit(solution)/shard_map/reduce_sum | solution.py:69
  440.6 13.0 %fusion.7 = f32[128,8,128]{2,1,0:T(8,128)S(1)} fusion(f32[128]{0:T(128)S(1)} %get-tuple-element.67, f32[128,128]{1,0:T(8,128)S(1)} %bitcast.171, f32[128,128]{1,0:T(8,128)S(1)} %bitcast.169, f32[128,128]{1,0:T(8,128)S(1)} %bitcast.173, f32[128,128]{1,0:T(8,128)S(1)} %get-tuple-element.55, f32[128,128]{1,0:T(8,128)S(1)} %get-tuple-element.56, ...), kind=kOutput, calls=%fused_computation.25 | convolution fusion | flops 56623104 | bytes 1180160 | tf_op jit(solution)/shard_map/rcj,rij->rci/dot_general | solution.py:66
  453.6 0.6 fusion.8
  455.0 4.3 collective-permute-start
  459.3 1.3 collective-permute-start.1
  460.6 3.2 collective-permute-done.1
  463.8 5.9 %collective-permute-start.2 = (f32[1,128]{1,0:T(1,128)S(1)}, f32[1,128]{1,0:T(1,128)S(1)}, u32[]{:S(2)}, u32[]{:S(2)}) collective-permute-start(f32[1,128]{1,0:T(1,128)S(1)} %get-tuple-element.59), channel_id=1, source_target_pairs={{0,16},{16,32},{32,48},{48,64},{64,80},{80,96},{96,112},{112,128},... | collective-permute-start | bytes 1544 | tf_op jit(solution)/shard_map/ppermute | solution.py:25
  469.7 1.9 collective-permute-start.3
  471.6 0.7 fusion.18
  472.3 4.4 collective-permute-done.3
  476.7 0.8 convolution_add_fusion
  (37 shorter events, 1.2 us)
Async XLA Ops:
  0.6 453.9 %copy-start = (bf16[1024,128]{1,0:T(8,128)(2,1)S(1)}, bf16[1024,128]{1,0:T(8,128)(2,1)}, u32[]{:S(2)}) copy-start(bf16[1024,128]{1,0:T(8,128)(2,1)} %param.16) | copy-start | bytes 786436
  2.9 19.0 %copy-start.5 = (s32[1,128,8]{1,2,0:T(8,128)S(1)}, s32[1,128,8]{1,2,0:T(8,128)}, u32[]{:S(2)}) copy-start(s32[1,128,8]{1,2,0:T(8,128)} %param.13) | copy-start | bytes 12292
  2.9 19.2 %copy-start.7 = (s32[1,128]{1,0:T(1,128)S(1)}, s32[1,128]{1,0:T(1,128)}, u32[]{:S(2)}) copy-start(s32[1,128]{1,0:T(1,128)} %param.15) | copy-start | bytes 1540
  2.9 19.2 %copy-start.6 = (s32[1,128]{1,0:T(1,128)S(1)}, s32[1,128]{1,0:T(1,128)}, u32[]{:S(2)}) copy-start(s32[1,128]{1,0:T(1,128)} %param.14) | copy-start | bytes 1540
  2.9 19.2 %copy-start.1 = (bf16[1,128,3,128]{3,1,2,0:T(8,128)(2,1)S(1)}, bf16[1,128,3,128]{3,1,2,0:T(8,128)(2,1)}, u32[]{:S(2)}) copy-start(bf16[1,128,3,128]{3,1,2,0:T(8,128)(2,1)} %param.10) | copy-start | bytes 294916
  6.8 264.2 %all-to-all-start = ((bf16[16,128,11,128]{3,1,2,0:T(8,128)(2,1)}), bf16[16,128,11,128]{3,1,2,0:T(8,128)(2,1)}, u32[]{:S(2)}, u32[]{:S(2)}) async-start(bf16[16,128,11,128]{3,1,2,0:T(8,128)(2,1)} %stack.2), calls=%async_computation | async-start | bytes 11534336 | tf_op jit(solution)/shard_map/all_to_all | solution.py:50
  440.6 13.7 %copy-start.2 = (f32[1,128,128]{2,1,0:T(8,128)S(1)}, f32[1,128,128]{2,1,0:T(8,128)}, u32[]{:S(2)}) copy-start(f32[1,128,128]{2,1,0:T(8,128)} %param.12) | copy-start | bytes 196612
  440.6 13.7 %copy-start.3 = (f32[1,128,128]{2,1,0:T(8,128)S(1)}, f32[1,128,128]{2,1,0:T(8,128)}, u32[]{:S(2)}) copy-start(f32[1,128,128]{2,1,0:T(8,128)} %param.11) | copy-start | bytes 196612
  440.6 36.1 %copy-start.4 = (f32[128,128]{1,0:T(8,128)S(1)}, f32[128,128]{1,0:T(8,128)}, u32[]{:S(2)}) copy-start(f32[128,128]{1,0:T(8,128)} %param.17) | copy-start | bytes 196612
  455.0 5.6 %collective-permute-start = (f32[32,128]{1,0:T(8,128)S(1)}, f32[32,128]{1,0:T(8,128)S(1)}, u32[]{:S(2)}, u32[]{:S(2)}) collective-permute-start(f32[32,128]{1,0:T(8,128)S(1)} %get-tuple-element.57), channel_id=1, source_target_pairs={{0,1},{1,2},{2,3},{3,4},{4,5},{5,6},{6,7},{7,8},{8,9},{9,10},{10,1... | collective-permute-start | bytes 49160 | tf_op jit(solution)/shard_map/ppermute | solution.py:15
  459.3 4.5 collective-permute-start.1
  463.8 8.5 %collective-permute-start.2 = (f32[1,128]{1,0:T(1,128)S(1)}, f32[1,128]{1,0:T(1,128)S(1)}, u32[]{:S(2)}, u32[]{:S(2)}) collective-permute-start(f32[1,128]{1,0:T(1,128)S(1)} %get-tuple-element.59), channel_id=1, source_target_pairs={{0,16},{16,32},{32,48},{48,64},{64,80},{80,96},{96,112},{112,128},... | collective-permute-start | bytes 1544 | tf_op jit(solution)/shard_map/ppermute | solution.py:25
  469.7 7.0 %collective-permute-start.3 = (f32[1,128]{1,0:T(1,128)S(1)}, f32[1,128]{1,0:T(1,128)S(1)}, u32[]{:S(2)}, u32[]{:S(2)}) collective-permute-start(f32[1,128]{1,0:T(1,128)S(1)} %get-tuple-element.60), channel_id=1, source_target_pairs={{16,0},{32,16},{48,32},{64,48},{80,64},{96,80},{112,96},{128,112},... | collective-permute-start | bytes 1544 | tf_op jit(solution)/shard_map/ppermute | solution.py:26
